TPU v7x, 32 devices: a whole 2x2x4 slice. The times are simulated.
32 devices in a mesh: section: 2 (over core), dp: 4 (over y, x), expert: 4 (over z).
Axes of the slice: x: 2, y: 2, z: 4, core: 2. Of those that a mesh axis runs over, the one named last changes fastest.
Arguments:
- tokens: bfloat16 [2, 64, 2048], P('section', 'expert'), may hold values from -6 to 6
- out_grad: bfloat16 [2, 64, 2048], P('section', 'expert'), may hold values from -6 to 6
- expert_ids: int32 [2, 64, 8], P('section', 'expert'), may hold values from 0 to 63, all different within a row; in each aligned block of 16 rows (0 to 15, 16 to 31, ..., all dimensions but the last counted through in order) at most 3 rows name the same one
- gates: bfloat16 [2, 64, 8], P('section', 'expert'), may hold values from 0.049804688 to 0.59765625
- w_gate: bfloat16 [2, 64, 2048, 1024], P('section', 'expert', None, 'dp'), may hold values from -0.125 to 0.125
- w_up: bfloat16 [2, 64, 2048, 1024], P('section', 'expert', None, 'dp'), may hold values from -0.125 to 0.125
- w_down: bfloat16 [2, 64, 1024, 2048], P('section', 'expert', 'dp'), may hold values from -0.1875 to 0.1875
Outputs:
- prev_grad: bfloat16 [2, 64, 2048], P('section', 'expert', 'dp')
- gate_grad: float32 [2, 64, 8], P('section', 'expert', 'dp')
- grad_w_gate: bfloat16 [2, 64, 2048, 1024], P('section', 'expert', None, 'dp')
- grad_w_up: bfloat16 [2, 64, 2048, 1024], P('section', 'expert', None, 'dp')
- grad_w_down: bfloat16 [2, 64, 1024, 2048], P('section', 'expert', 'dp')
Inputs may be any that keep to these rules, and one draw needn't show every extreme that they name: `expert_ids`: each token names 8 different experts; within one section, the 16 tokens of one index of expert name any one expert at most 3 times.
All inputs are finite; a program needn't handle non-finite values.
Results may differ from a plain program's by a relative error of at most 0.0057.
Values may be sent and summed in bfloat16 or wider, within the bound.
A program may use at most 192 MiB of HBM per device.

v0:
```python
import jax
import jax.numpy as jnp
from jax import lax
from jax.sharding import PartitionSpec as P

CAP = 3


def from_behind(value, axis, steps):
    count = lax.axis_size(axis)
    pairs = [(source, (source + steps) % count) for source in range(count)]
    return lax.ppermute(value, axis, pairs)


def expert_backward(xs, dys, gs, wg, wu, wd):
    a = jnp.dot(xs, wg, preferred_element_type=jnp.float32)
    b = jnp.dot(xs, wu, preferred_element_type=jnp.float32)
    sig = jax.nn.sigmoid(a)
    silu = a * sig
    hid = silu * b
    dz = jnp.dot(dys, wd.T, preferred_element_type=jnp.float32)
    gate_f = gs.astype(jnp.float32)[:, None]
    dgate = jnp.sum(hid * dz, axis=1)
    dh = gate_f * dz
    db = (dh * silu).astype(jnp.bfloat16)
    da = (dh * b * sig * (1.0 + a * (1.0 - sig))).astype(jnp.bfloat16)
    hid_b = hid.astype(jnp.bfloat16)
    dout = (gate_f * dys.astype(jnp.float32)).astype(jnp.bfloat16)
    dwg = jnp.dot(xs.T, da, preferred_element_type=jnp.float32)
    dwu = jnp.dot(xs.T, db, preferred_element_type=jnp.float32)
    dwd = jnp.dot(hid_b.T, dout, preferred_element_type=jnp.float32)
    dxp = jnp.dot(da, wg.T, preferred_element_type=jnp.float32) + jnp.dot(
        db, wu.T, preferred_element_type=jnp.float32
    )
    return (dxp, dgate, dwg, dwu, dwd)


def local(tokens, out_grad, expert_ids, gates, w_gate, w_up, w_down):
    x_local = tokens[0]
    dy_local = out_grad[0]
    ids = expert_ids[0]
    tok_dev, top = ids.shape
    n_exp = lax.axis_size("expert")
    exp_loc = w_gate.shape[1]
    experts = exp_loc * n_exp
    slots = experts * CAP
    flat = ids.reshape(-1)
    onehot = (flat[:, None] == jnp.arange(experts, dtype=jnp.int32)[None, :]).astype(jnp.int32)
    rank = jnp.sum((jnp.cumsum(onehot, axis=0) - onehot) * onehot, axis=1)
    slot_of = flat * CAP + rank
    pair_map = (slot_of[:, None] == jnp.arange(slots, dtype=jnp.int32)[None, :]).astype(jnp.float32)
    token_map = jnp.sum(pair_map.reshape(tok_dev, top, slots), axis=1)
    token_map_b = token_map.astype(jnp.bfloat16)
    gate_slots = jnp.dot(
        gates[0].reshape(-1).astype(jnp.float32), pair_map, precision=lax.Precision.HIGHEST
    ).astype(jnp.bfloat16)
    x_slots = jnp.dot(token_map_b.T, x_local, preferred_element_type=jnp.float32).astype(
        jnp.bfloat16
    )
    dy_slots = jnp.dot(token_map_b.T, dy_local, preferred_element_type=jnp.float32).astype(
        jnp.bfloat16
    )
    recv_x, recv_dy, recv_gate = (
        lax.all_to_all(x_slots, "expert", split_axis=0, concat_axis=0, tiled=True),
        lax.all_to_all(dy_slots, "expert", split_axis=0, concat_axis=0, tiled=True),
        lax.all_to_all(gate_slots, "expert", split_axis=0, concat_axis=0, tiled=True),
    )

    def to_experts(arr):
        rest = arr.shape[1:]
        shaped = arr.reshape((n_exp, exp_loc, CAP) + rest)
        return jnp.swapaxes(shaped, 0, 1).reshape((exp_loc, n_exp * CAP) + rest)

    def from_experts(arr):
        rest = arr.shape[2:]
        shaped = arr.reshape((exp_loc, n_exp, CAP) + rest)
        return jnp.swapaxes(shaped, 0, 1).reshape((slots,) + rest)

    def per_expert(operands):
        return expert_backward(*operands)

    dxp, dgp, dwg, dwu, dwd = lax.map(
        per_expert,
        (
            to_experts(recv_x),
            to_experts(recv_dy),
            to_experts(recv_gate),
            w_gate[0],
            w_up[0],
            w_down[0],
        ),
    )
    dx_slot = from_experts(dxp)
    dg_slot = from_experts(dgp)
    back_dx, back_dg = (
        lax.all_to_all(dx_slot, "expert", split_axis=0, concat_axis=0, tiled=True),
        lax.all_to_all(dg_slot, "expert", split_axis=0, concat_axis=0, tiled=True),
    )
    dx_full = jnp.dot(token_map, back_dx, precision=lax.Precision.HIGHEST)
    dg_pairs = jnp.dot(pair_map, back_dg, precision=lax.Precision.HIGHEST).reshape(tok_dev, top)
    dx_token, dg_token = (
        lax.psum_scatter(dx_full, "dp", scatter_dimension=1, tiled=True),
        lax.psum_scatter(dg_pairs, "dp", scatter_dimension=1, tiled=True),
    )
    arrived = from_behind(dx_token.astype(jnp.bfloat16), "section", -1)
    return (
        arrived[None],
        dg_token[None],
        dwg.astype(jnp.bfloat16)[None],
        dwu.astype(jnp.bfloat16)[None],
        dwd.astype(jnp.bfloat16)[None],
    )


def solution(mesh):
    placed = (
        P("section", "expert", None),
        P("section", "expert", None),
        P("section", "expert", None),
        P("section", "expert", None),
        P("section", "expert", None, "dp"),
        P("section", "expert", None, "dp"),
        P("section", "expert", "dp", None),
    )
    return jax.shard_map(
        local,
        mesh=mesh,
        in_specs=placed,
        out_specs=(
            P("section", "expert", "dp"),
            P("section", "expert", "dp"),
            P("section", "expert", None, "dp"),
            P("section", "expert", None, "dp"),
            P("section", "expert", "dp", None),
        ),
        check_vma=False,
    )
```

profile of v0, /device:TPU:0, one launch (start us, length us, event | category | flops | bytes accessed | tf_op | source)
XLA Modules:
  0.0 392.6 jit_solution(13189627752245280733)
XLA Ops:
  10.3 6.3 %all-to-all-start = ((bf16[4,48,1]{1,2,0:T(2,128)(2,1)}), bf16[4,48,1]{1,2,0:T(2,128)(2,1)S(1)}, u32[]{:S(2)}, u32[]{:S(2)}) async-start(bf16[4,48,1]{1,2,0:T(2,128)(2,1)} %all_to_all.46), calls=%async_computation | async-start | bytes 4096 | tf_op jit(solution)/shard_map/all_to_all | solution.py:66
  18.9 3.1 all-to-all-done
  22.1 3.5 all-to-all-start.1
  27.7 16.8 %all-to-all-done.1 = bf16[4,48,2048]{2,1,0:T(8,128)(2,1)S(1)} async-done(((bf16[4,48,2048]{2,1,0:T(8,128)(2,1)}), bf16[4,48,2048]{2,1,0:T(8,128)(2,1)S(1)}, u32[]{:S(2)}, u32[]{:S(2)}) %all-to-all-start.1) | async-done | bytes 786464 | tf_op jit(solution)/shard_map/all_to_all | solution.py:65
  44.5 3.5 all-to-all-start.2
  49.9 17.6 %all-to-all-done.2 = bf16[4,48,2048]{2,1,0:T(8,128)(2,1)S(1)} async-done(((bf16[4,48,2048]{2,1,0:T(8,128)(2,1)}), bf16[4,48,2048]{2,1,0:T(8,128)(2,1)S(1)}, u32[]{:S(2)}, u32[]{:S(2)}) %all-to-all-start.2) | async-done | bytes 786464 | tf_op jit(solution)/shard_map/all_to_all | solution.py:64
  69.1 247.2 %while.18 = (s32[]{:T(128)}, f32[16,12,2048]{2,0,1:T(8,128)}, f32[16,12]{1,0:T(8,128)S(1)}, bf16[16,2048,256]{2,1,0:T(8,128)(2,1)}, bf16[16,2048,256]{2,1,0:T(8,...) while((s32[]{:T(128)}, f32[16,12,2048]{2,0,1:T(8,128)}, ...), condition=%wide.region_5.6_spmd, body=%wide.region_3.5_spmd.sunk | while | flops 100832256 | bytes 12755305 | solution.py:82
  81.5 3.0 dynamic_update_slice.30
  96.9 3.0 dynamic_update_slice.30
  112.4 3.0 dynamic_update_slice.30
  127.8 3.0 dynamic_update_slice.30
  143.3 3.0 dynamic_update_slice.30
  158.7 3.0 dynamic_update_slice.30
  174.2 3.0 dynamic_update_slice.30
  189.6 3.0 dynamic_update_slice.30
  205.1 3.0 dynamic_update_slice.30
  220.5 3.0 dynamic_update_slice.30
  236.0 3.0 dynamic_update_slice.30
  266.9 3.0 dynamic_update_slice.30
  297.8 3.0 dynamic_update_slice.30
  319.6 39.0 %all_to_all.52 = f32[4,48,2048]{2,1,0:T(8,128)S(1)} all-to-all(f32[4,48,2048]{2,1,0:T(8,128)S(1)} %copy.89), channel_id=1, replica_groups=mesh['section'=2,'dp'=4,'expert'=4] {'expert'}, dimensions={0} | all-to-all | bytes 3145728 | tf_op jit(solution)/shard_map/all_to_all | solution.py:96
  361.0 3.2 all-to-all-start.4
  365.5 4.2 %all-to-all-done.4 = f32[4,48,1]{1,2,0:T(1,128)S(1)} async-done(((f32[4,48,1]{1,2,0:T(1,128)}), f32[4,48,1]{1,2,0:T(1,128)S(1)}, u32[]{:S(2)}, u32[]{:S(2)}) %all-to-all-start.4) | async-done | bytes 800 | tf_op jit(solution)/shard_map/all_to_all | solution.py:97
  371.6 9.9 %all-reduce = f32[16,8]{0,1:T(8,128)S(1)} all-reduce(f32[16,8]{0,1:T(8,128)S(1)} %bitcast.168), channel_id=3, replica_groups=mesh['section'=2,'dp'=4,'expert'=4] {'dp'}, use_global_device_ids=true, to_apply=%region_7.8.clone | all-reduce | flops 128 | bytes 1024
  (240 shorter events, 230.8 us)
Async XLA Ops:
  7.2 10.5 %copy-start = (bf16[1,16,2048]{2,1,0:T(8,128)(2,1)S(1)}, bf16[1,16,2048]{2,1,0:T(8,128)(2,1)}, u32[]{:S(2)}) copy-start(bf16[1,16,2048]{2,1,0:T(8,128)(2,1)} %param.10) | copy-start | bytes 196612
  10.3 11.8 %all-to-all-start = ((bf16[4,48,1]{1,2,0:T(2,128)(2,1)}), bf16[4,48,1]{1,2,0:T(2,128)(2,1)S(1)}, u32[]{:S(2)}, u32[]{:S(2)}) async-start(bf16[4,48,1]{1,2,0:T(2,128)(2,1)} %all_to_all.46), calls=%async_computation | async-start | bytes 4096 | tf_op jit(solution)/shard_map/all_to_all | solution.py:66
  22.1 22.4 %all-to-all-start.1 = ((bf16[4,48,2048]{2,1,0:T(8,128)(2,1)}), bf16[4,48,2048]{2,1,0:T(8,128)(2,1)S(1)}, u32[]{:S(2)}, u32[]{:S(2)}) async-start(bf16[4,48,2048]{2,1,0:T(8,128)(2,1)} %bitcast.16), calls=%async_computation.1 | async-start | bytes 1572864 | tf_op jit(solution)/shard_map/all_to_all | solution.py:65
  44.5 23.1 %all-to-all-start.2 = ((bf16[4,48,2048]{2,1,0:T(8,128)(2,1)}), bf16[4,48,2048]{2,1,0:T(8,128)(2,1)S(1)}, u32[]{:S(2)}, u32[]{:S(2)}) async-start(bf16[4,48,2048]{2,1,0:T(8,128)(2,1)} %bitcast.22), calls=%async_computation.2 | async-start | bytes 1572864 | tf_op jit(solution)/shard_map/all_to_all | solution.py:64
  48.0 335.2 %reduce-scatter.2.cloned.1.call-start = ((), (), s32[]{:S(2)}) async-start(), calls=%async_computation.6 | async-start | bytes 163840 | tf_op jit(solution)/shard_map/reduce_scatter | solution.py:102
  69.1 295.2 %copy-start.2 = (u32[32]{0:T(128)S(1)}, u32[32]{0:T(128)}, u32[]{:S(2)}) copy-start(u32[32]{0:T(128)} %constant.51) | copy-start | bytes 388
  316.3 69.5 %copy-start.1 = (bf16[1,16,2048]{2,1,0:T(8,128)(2,1)S(1)}, bf16[1,16,2048]{2,1,0:T(8,128)(2,1)}, u32[]{:S(2)}) copy-start(bf16[1,16,2048]{2,1,0:T(8,128)(2,1)} %param.10) | copy-start | bytes 196612
  361.0 8.7 %all-to-all-start.4 = ((f32[4,48,1]{1,2,0:T(1,128)}), f32[4,48,1]{1,2,0:T(1,128)S(1)}, u32[]{:S(2)}, u32[]{:S(2)}) async-start(f32[4,48,1]{1,2,0:T(1,128)} %bitcast.35), calls=%async_computation.5 | async-start | bytes 4096 | tf_op jit(solution)/shard_map/all_to_all | solution.py:97
  383.9 1.2 collective-permute-start
Sparse Core Ops, SparseCore 0:
  360.2 22.8 reduce-scatter.1
where the time goes:
time: 397 us; the launch traced here: 393 us
  matrix products  202 us (51%)
  local copies, waits for them, and re-layouts  63.3 us (16%)
  blocking collectives  48.9 us (12%)
  waiting for transfers between devices  44 us (11%)
  starting transfers between devices  16.6 us (4%)
  between operations  14.9 us (4%)
    dynamic_update_slice x48, local copies, waits for them, and re-layouts, local(): lax.map(per_expert, (to_experts(recv_x), to_experts(recv_dy), to_experts(...  50.7 us
    all_to_all x1, blocking collectives, local(): lax.all_to_all(dx_slot, 'expert', split_axis=0, concat_axis=0, tiled=True)  39 us
    dot_general x16, matrix products, expert_backward(): dz = jnp.dot(dys, wd.T, preferred_element_type=jnp.float32)  27.7 us
    dot_general x16, matrix products, expert_backward(): jnp.dot(db, wu.T, preferred_element_type=jnp.float32)  25.8 us
    dot_general x16, matrix products, expert_backward(): jnp.dot(da, wg.T, preferred_element_type=jnp.float32)  25.5 us
    dot_general x16, matrix products, expert_backward(): b = jnp.dot(xs, wu, preferred_element_type=jnp.float32)  23.6 us
    dot_general x16, matrix products, expert_backward(): a = jnp.dot(xs, wg, preferred_element_type=jnp.float32)  23.6 us
    dot_general x16, matrix products, expert_backward(): dwg = jnp.dot(xs.T, da, preferred_element_type=jnp.float32)  23.4 us
  transfers between devices with their start and end apart: 6, of which 6 were waited for; matrix products, arithmetic and copies ran while one was open for 2% of the time, Pallas kernels for 0%

commit v1 on v0

--- a/solution.py
+++ b/solution.py
@@ -4,6 +4,31 @@
 from jax.sharding import PartitionSpec as P
 
 CAP = 3
+
+
+def cut_along(shard, dim, length):
+    shape = shard.shape
+    pieces = shard.reshape(*shape[:dim], length, shape[dim] // length, *shape[dim + 1 :])
+    return jnp.moveaxis(pieces, dim, 0)
+
+
+def joined_along(blocks, dim):
+    blocks = jnp.moveaxis(blocks, 0, dim)
+    dims = blocks.shape
+    return blocks.reshape(*dims[:dim], dims[dim] * dims[dim + 1], *dims[dim + 2 :])
+
+
+def exchange_directly(x, axis, split_dim, concat_dim):
+    devices, index = (lax.axis_size(axis), lax.axis_index(axis))
+    blocks = cut_along(x, split_dim, devices)
+    finished = [blocks[index]]
+    for step in range(1, devices):
+        sent = blocks[(index + step) % devices]
+        finished.append(
+            lax.ppermute(sent, axis, [(i, (i + step) % devices) for i in range(devices)])
+        )
+    blocks = jnp.stack(finished)[(index - jnp.arange(devices)) % devices]
+    return joined_along(blocks, concat_dim)
 
 
 def from_behind(value, axis, steps):
@@ -61,7 +86,7 @@
         jnp.bfloat16
     )
     recv_x, recv_dy, recv_gate = (
-        lax.all_to_all(x_slots, "expert", split_axis=0, concat_axis=0, tiled=True),
+        exchange_directly(x_slots, "expert", 0, 0),
         lax.all_to_all(dy_slots, "expert", split_axis=0, concat_axis=0, tiled=True),
         lax.all_to_all(gate_slots, "expert", split_axis=0, concat_axis=0, tiled=True),
     )

time: 397 us -> 392 us (0.987)
  waiting for transfers between devices: 44 us -> 34.8 us
    ppermute x0 -> x3, waiting for transfers between devices: none -> 25.1 us  [exchange_directly(): lax.ppermute(sent, axis, [(i, (i + step) % devices) for i in range(device...]
    all_to_all x1 -> x0, waiting for transfers between devices: 17.6 us -> none  [local(): lax.all_to_all(x_slots, 'expert', split_axis=0, concat_axis=0, tiled=True)]
    all_to_all x1, waiting for transfers between devices: 16.8 us -> 0.01 us  [local(): lax.all_to_all(dy_slots, 'expert', split_axis=0, concat_axis=0, tiled=True)]
    ppermute x0 -> x3, starting transfers between devices: none -> 5.77 us  [exchange_directly(): lax.ppermute(sent, axis, [(i, (i + step) % devices) for i in range(device...]
  transfers between devices with their start and end apart: 6 -> 8, of which waited for: 6 -> 6; matrix products, arithmetic and copies ran while one was open for 2% -> 2% of each run, Pallas kernels for 0% -> 0%
where the time goes in v1:
time: 392 us; the launch traced here: 388 us
  matrix products  201 us (51%)
  local copies, waits for them, and re-layouts  64 us (16%)
  blocking collectives  50.9 us (13%)
  waiting for transfers between devices  34.8 us (9%)
  starting transfers between devices  18.8 us (5%)
  between operations  14.9 us (4%)
    dynamic_update_slice x48, local copies, waits for them, and re-layouts, local(): lax.map(per_expert, (to_experts(recv_x), to_experts(recv_dy), to_experts(...  50.7 us
    all_to_all x1, blocking collectives, local(): lax.all_to_all(dx_slot, 'expert', split_axis=0, concat_axis=0, tiled=True)  41 us
    dot_general x16, matrix products, expert_backward(): dz = jnp.dot(dys, wd.T, preferred_element_type=jnp.float32)  27.7 us
    dot_general x16, matrix products, expert_backward(): jnp.dot(db, wu.T, preferred_element_type=jnp.float32)  25.8 us
    dot_general x16, matrix products, expert_backward(): jnp.dot(da, wg.T, preferred_element_type=jnp.float32)  25.5 us
    ppermute x3, waiting for transfers between devices, exchange_directly(): lax.ppermute(sent, axis, [(i, (i + step) % devices) for i in range(device...  25.1 us
    dot_general x16, matrix products, expert_backward(): a = jnp.dot(xs, wg, preferred_element_type=jnp.float32)  23.6 us
    dot_general x16, matrix products, expert_backward(): b = jnp.dot(xs, wu, preferred_element_type=jnp.float32)  23.6 us
  transfers between devices with their start and end apart: 8, of which 6 were waited for; matrix products, arithmetic and copies ran while one was open for 2% of the time, Pallas kernels for 0%

profile of v1, /device:TPU:0, one launch (start us, length us, event | category | flops | bytes accessed | tf_op | source)
XLA Modules:
  0.0 387.5 jit_solution(3972315570855143757)
XLA Ops:
  10.3 6.3 %all-to-all-start = ((bf16[4,48,1]{1,2,0:T(2,128)(2,1)}), bf16[4,48,1]{1,2,0:T(2,128)(2,1)S(1)}, u32[]{:S(2)}, u32[]{:S(2)}) async-start(bf16[4,48,1]{1,2,0:T(2,128)(2,1)} %all_to_all.38), calls=%async_computation | async-start | bytes 4096 | tf_op jit(solution)/shard_map/all_to_all | solution.py:91
  18.9 3.1 all-to-all-done
  22.1 3.5 all-to-all-start.1
  33.1 14.9 %collective-permute-done = bf16[48,2048]{1,0:T(8,128)(2,1)S(1)} collective-permute-done((bf16[48,2048]{1,0:T(8,128)(2,1)S(1)}, bf16[48,2048]{1,0:T(8,128)(2,1)S(1)}, u32[]{:S(2)}, u32[]{:S(2)}) %collective-permute-start) | collective-permute-done | bytes 196640 | tf_op jit(solution)/shard_map/ppermute | solution.py:28
  48.0 10.2 %collective-permute-done.1 = bf16[48,2048]{1,0:T(8,128)(2,1)S(1)} collective-permute-done((bf16[48,2048]{1,0:T(8,128)(2,1)S(1)}, bf16[48,2048]{1,0:T(8,128)(2,1)S(1)}, u32[]{:S(2)}, u32[]{:S(2)}) %collective-permute-start.1) | collective-permute-done | bytes 196640 | tf_op jit(solution)/shard_map/ppermute | solution.py:28
  62.0 247.2 %while.18 = (s32[]{:T(128)}, f32[16,12,2048]{2,0,1:T(8,128)}, f32[16,12]{1,0:T(8,128)S(1)}, bf16[16,2048,256]{2,1,0:T(8,128)(2,1)}, bf16[16,2048,256]{2,1,0:T(8,...) while((s32[]{:T(128)}, f32[16,12,2048]{2,0,1:T(8,128)}, ...), condition=%wide.region_5.6_spmd, body=%wide.region_3.5_spmd.sunk | while | flops 100832256 | bytes 12755305 | solution.py:107
  74.4 3.0 dynamic_update_slice.30
  89.8 3.0 dynamic_update_slice.30
  105.3 3.0 dynamic_update_slice.30
  120.7 3.0 dynamic_update_slice.30
  136.2 3.0 dynamic_update_slice.30
  151.6 3.0 dynamic_update_slice.30
  167.1 3.0 dynamic_update_slice.30
  182.5 3.0 dynamic_update_slice.30
  198.0 3.0 dynamic_update_slice.30
  213.4 3.0 dynamic_update_slice.30
  228.9 3.0 dynamic_update_slice.30
  244.3 3.0 dynamic_update_slice.30
  275.2 3.0 dynamic_update_slice.30
  306.1 3.0 dynamic_update_slice.30
  312.5 41.0 %all_to_all.43 = f32[4,48,2048]{2,1,0:T(8,128)S(1)} all-to-all(f32[4,48,2048]{2,1,0:T(8,128)S(1)} %copy.88), channel_id=1, replica_groups=mesh['section'=2,'dp'=4,'expert'=4] {'expert'}, dimensions={0} | all-to-all | bytes 3145728 | tf_op jit(solution)/shard_map/all_to_all | solution.py:121
  355.9 3.2 all-to-all-start.3
  360.4 4.2 %all-to-all-done.3 = f32[4,48,1]{1,2,0:T(1,128)S(1)} async-done(((f32[4,48,1]{1,2,0:T(1,128)}), f32[4,48,1]{1,2,0:T(1,128)S(1)}, u32[]{:S(2)}, u32[]{:S(2)}) %all-to-all-start.3) | async-done | bytes 800 | tf_op jit(solution)/shard_map/all_to_all | solution.py:122
  366.5 9.9 %all-reduce = f32[16,8]{0,1:T(8,128)S(1)} all-reduce(f32[16,8]{0,1:T(8,128)S(1)} %bitcast.183), channel_id=3, replica_groups=mesh['section'=2,'dp'=4,'expert'=4] {'dp'}, use_global_device_ids=true, to_apply=%region_7.8.clone | all-reduce | flops 128 | bytes 1024
  (249 shorter events, 233.5 us)
Async XLA Ops:
  7.2 10.5 %copy-start = (bf16[1,16,2048]{2,1,0:T(8,128)(2,1)S(1)}, bf16[1,16,2048]{2,1,0:T(8,128)(2,1)}, u32[]{:S(2)}) copy-start(bf16[1,16,2048]{2,1,0:T(8,128)(2,1)} %param.10) | copy-start | bytes 196612
  10.3 11.8 %all-to-all-start = ((bf16[4,48,1]{1,2,0:T(2,128)(2,1)}), bf16[4,48,1]{1,2,0:T(2,128)(2,1)S(1)}, u32[]{:S(2)}, u32[]{:S(2)}) async-start(bf16[4,48,1]{1,2,0:T(2,128)(2,1)} %all_to_all.38), calls=%async_computation | async-start | bytes 4096 | tf_op jit(solution)/shard_map/all_to_all | solution.py:91
  22.1 38.4 %all-to-all-start.1 = ((bf16[4,48,2048]{2,1,0:T(8,128)(2,1)}), bf16[4,48,2048]{2,1,0:T(8,128)(2,1)S(1)}, u32[]{:S(2)}, u32[]{:S(2)}) async-start(bf16[4,48,2048]{2,1,0:T(8,128)(2,1)} %bitcast.16), calls=%async_computation.1 | async-start | bytes 1572864 | tf_op jit(solution)/shard_map/all_to_all | solution.py:90
  25.6 352.6 %reduce-scatter.2.cloned.1.call-start = ((), (), s32[]{:S(2)}) async-start(), calls=%async_computation.5 | async-start | bytes 163840 | tf_op jit(solution)/shard_map/reduce_scatter | solution.py:127
  27.0 21.1 %collective-permute-start = (bf16[48,2048]{1,0:T(8,128)(2,1)S(1)}, bf16[48,2048]{1,0:T(8,128)(2,1)S(1)}, u32[]{:S(2)}, u32[]{:S(2)}) collective-permute-start(bf16[48,2048]{1,0:T(8,128)(2,1)S(1)} %get-tuple-element.154), channel_id=1, source_target_pairs={{0,1},{1,2},{2,3},{3,0},{4,5},{5,6},{6,7},{7,4},{8,9},{9,10},{10,1... | collective-permute-start | bytes 589832 | tf_op jit(solution)/shard_map/ppermute | solution.py:28
  28.9 29.3 %collective-permute-start.1 = (bf16[48,2048]{1,0:T(8,128)(2,1)S(1)}, bf16[48,2048]{1,0:T(8,128)(2,1)S(1)}, u32[]{:S(2)}, u32[]{:S(2)}) collective-permute-start(bf16[48,2048]{1,0:T(8,128)(2,1)S(1)} %get-tuple-element.153), channel_id=1, source_target_pairs={{0,2},{1,3},{2,0},{3,1},{4,6},{5,7},{6,4},{7,5},{8,10},{9,11},{10,... | collective-permute-start | bytes 589832 | tf_op jit(solution)/shard_map/ppermute | solution.py:28
  31.3 26.9 %collective-permute-start.2 = (bf16[48,2048]{1,0:T(8,128)(2,1)S(1)}, bf16[48,2048]{1,0:T(8,128)(2,1)S(1)}, u32[]{:S(2)}, u32[]{:S(2)}) collective-permute-start(bf16[48,2048]{1,0:T(8,128)(2,1)S(1)} %get-tuple-element.152), channel_id=1, source_target_pairs={{0,3},{1,0},{2,1},{3,2},{4,7},{5,4},{6,5},{7,6},{8,11},{9,8},{10,9... | collective-permute-start | bytes 589832 | tf_op jit(solution)/shard_map/ppermute | solution.py:28
  61.9 297.2 %copy-start.2 = (u32[32]{0:T(128)S(1)}, u32[32]{0:T(128)}, u32[]{:S(2)}) copy-start(u32[32]{0:T(128)} %constant.89) | copy-start | bytes 388
  309.1 71.6 %copy-start.1 = (bf16[1,16,2048]{2,1,0:T(8,128)(2,1)S(1)}, bf16[1,16,2048]{2,1,0:T(8,128)(2,1)}, u32[]{:S(2)}) copy-start(bf16[1,16,2048]{2,1,0:T(8,128)(2,1)} %param.10) | copy-start | bytes 196612
  355.9 8.7 %all-to-all-start.3 = ((f32[4,48,1]{1,2,0:T(1,128)}), f32[4,48,1]{1,2,0:T(1,128)S(1)}, u32[]{:S(2)}, u32[]{:S(2)}) async-start(f32[4,48,1]{1,2,0:T(1,128)} %bitcast.42), calls=%async_computation.4 | async-start | bytes 4096 | tf_op jit(solution)/shard_map/all_to_all | solution.py:122
  378.9 1.2 collective-permute-start.3
Sparse Core Ops, SparseCore 0:
  355.1 22.9 reduce-scatter.1
